TPU v7x, 256 devices: a whole 4x4x8 slice. The times are simulated.
256 devices in a mesh: cont: 8 (over z), line: 8 (over y, core), scen: 4 (over x).
Axes of the slice: x: 4, y: 4, z: 8, core: 2. Of those that a mesh axis runs over, the one named last changes fastest.
Arguments:
- lodf: bfloat16 [1024, 4096], P('line', 'cont'), may hold values from -1 to 1
- flow: float32 [1024, 256], P('line', 'scen'), may hold values from -6 to 6
- out_flow: float32 [256, 4096], P('scen', 'cont'), may hold values from -6 to 6
- limits: float32 [1024], P('line'), may hold values from 0.5 to 2
- ptdf_mon: bfloat16 [1024, 2048], P('line'), may hold values from -6 to 6
- ptdf_out: bfloat16 [4096, 2048], P('cont'), may hold values from -6 to 6
- viol_cont: int32 [131072], P(('cont', 'line', 'scen')), may hold values from 0 to 511
- viol_line: int32 [131072], P(('cont', 'line', 'scen')), may hold values from 0 to 127
- viol_scen: int32 [131072], P(('cont', 'line', 'scen')), may hold values from 0 to 63
- rows_used: int32 [256], P(('cont', 'line', 'scen')), may hold values from 64 to 512, as said below
Outputs:
- worst: float32 [1024, 256], P('line', 'scen')
- schur: float32 [2048, 2048], P(('line', 'scen'))
Inputs may be any that keep to these rules, and one draw needn't show every extreme that they name: `rows_used`: each device uses a leading run of its 512 slots; the counts are skewed, and some device is full.
All inputs are finite; a program needn't handle non-finite values.
Results may differ from a plain program's by a relative error of at most 0.00096.
Values may be sent and summed in bfloat16 or wider, within the bound.
No kernel may reach another device: no remote copies, remote signals or barrier semaphores. Data moves between devices by JAX's collectives and lax.ppermute only.
A program may use at most 128 MiB of HBM per device.

v0:
```python
import math
import jax
import jax.numpy as jnp
from jax import lax
from jax.sharding import PartitionSpec as P


def local(
    lodf, flow, out_flow, limits, ptdf_mon, ptdf_out, viol_cont, viol_line, viol_scen, rows_used
):
    line_dev, cont_dev = lodf.shape
    scen_dev = flow.shape[1]
    width = ptdf_mon.shape[1]
    n_rows = viol_cont.shape[0]
    n_cont = lax.axis_size("cont")
    n_line = lax.axis_size("line")
    n_scen = lax.axis_size("scen")
    owners = n_line * n_scen
    devices = n_cont * owners
    row_block = math.gcd(n_rows, 512)
    lines_each = math.gcd(line_dev, 32)

    def screen(pair):
        lodf_block, flow_block = pair
        post = (
            flow_block[:, :, None]
            + lodf_block.astype(jnp.float32)[:, None, :] * out_flow[None, :, :]
        )
        return jnp.max(jnp.abs(post), axis=2)

    local_worst = lax.map(
        screen,
        (
            lodf.reshape(line_dev // lines_each, lines_each, cont_dev),
            flow.reshape(line_dev // lines_each, lines_each, scen_dev),
        ),
    ).reshape(line_dev, scen_dev)
    worst = lax.pmax(local_worst, "cont") / limits[:, None]
    coef = lodf[viol_line, viol_cont].astype(jnp.float32)
    rows = (
        ptdf_mon[viol_line].astype(jnp.float32)
        + coef[:, None] * ptdf_out[viol_cont].astype(jnp.float32)
    ).astype(jnp.bfloat16)
    rows = lax.optimization_barrier(rows)
    post = flow[viol_line, viol_scen] + coef * out_flow[viol_scen, viol_cont]
    ratio = post / limits[viol_line]
    live = jnp.arange(n_rows, dtype=jnp.int32) < rows_used[0]
    weight = jnp.where(live, 1.0 + ratio * ratio, jnp.zeros_like(ratio))
    scaled = (weight[:, None] * rows.astype(jnp.float32)).astype(jnp.bfloat16)
    trips = (rows_used[0] + row_block - 1) // row_block
    row_blocks = rows.reshape(n_rows // row_block, row_block, width)
    scaled_blocks = scaled.reshape(n_rows // row_block, row_block, width)

    def step(index, acc):
        row_tile = lax.dynamic_index_in_dim(row_blocks, index, 0, keepdims=False)
        scaled_tile = lax.dynamic_index_in_dim(scaled_blocks, index, 0, keepdims=False)
        return acc + lax.dot_general(
            row_tile, scaled_tile, (((0,), (0,)), ((), ())), preferred_element_type=jnp.float32
        )

    owned = lax.psum_scatter(
        lax.fori_loop(
            0,
            trips,
            step,
            jnp.zeros((lax.axis_size(("line", "scen")) * (width // owners), width), jnp.float32),
        ),
        ("line", "scen"),
        scatter_dimension=0,
        tiled=True,
    )
    total = lax.psum(owned, "cont")
    schur = total * (1.0 / (n_rows * devices))
    return (worst, schur)


def solution(mesh):
    in_specs = (
        P("line", "cont"),
        P("line", "scen"),
        P("scen", "cont"),
        P("line"),
        P("line", None),
        P("cont", None),
        P(("cont", "line", "scen")),
        P(("cont", "line", "scen")),
        P(("cont", "line", "scen")),
        P(("cont", "line", "scen")),
    )
    out_specs = (P("line", "scen"), P(("line", "scen"), None))
    return jax.shard_map(local, mesh=mesh, in_specs=in_specs, out_specs=out_specs, check_vma=False)
```

profile of v0, /device:TPU:2, one launch (start us, length us, event | category | flops | bytes accessed | tf_op | source)
XLA Modules:
  0.0 275.0 jit_solution(17831814919024099587)
XLA Ops:
  7.2 0.0 reduce-scatter.2.cloned.1.call-start
  8.1 0.7 shift-left_or_fusion
  8.8 5.2 %gather_fusion.1 = bf16[512]{0:T(512)(128)(2,1)S(1)} fusion(bf16[128,512]{1,0:T(8,128)(2,1)} %param.14, s32[512]{0:T(512)S(1)} %get-tuple-element.84), kind=kCustom, calls=%fused_computation.1 | custom fusion | bytes 6144 | tf_op jit(solution)/shard_map/gather | solution.py:39
  14.0 3.3 %gather_fusion = bf16[512,2048]{1,0:T(8,128)(2,1)} fusion(bf16[128,2048]{1,0:T(8,128)(2,1)S(1)} %copy-done.2, s32[1024]{0:T(1024)S(1)} %get-tuple-element.89), kind=kCustom, calls=%fused_computation | custom fusion | bytes 4196352 | tf_op jit(solution)/shard_map/gather | solution.py:41
  17.3 3.3 %gather_fusion.2 = bf16[512,2048]{1,0:T(8,128)(2,1)} fusion(bf16[512,2048]{1,0:T(8,128)(2,1)S(1)} %copy-done, s32[1024]{0:T(1024)S(1)} %get-tuple-element.88), kind=kCustom, calls=%fused_computation.2 | custom fusion | bytes 4196352 | tf_op jit(solution)/shard_map/gather | solution.py:42
  20.6 4.2 %add_convert_fusion = bf16[512,2048]{1,0:T(8,128)(2,1)} fusion(bf16[512,2048]{1,0:T(8,128)(2,1)} %gather_fusion.2, bf16[512,2048]{1,0:T(8,128)(2,1)} %gather_fusion, f32[512]{0:T(512)S(1)} %convert_element_type.36), kind=kLoop, calls=%fused_computation.14 | loop fusion | flops 5242880 | bytes 6293504 | tf_op jit(solution)/shard_map/convert_element_type | solution.py:43
  24.8 3.3 %gather_fusion.5 = f32[512]{0:T(512)S(1)} fusion(f32[128]{0:T(128)S(1)} %copy-done.1, s32[1024]{0:T(1024)S(1)} %get-tuple-element.89), kind=kCustom, calls=%fused_computation.5 | custom fusion | bytes 6144 | tf_op jit(solution)/shard_map/gather | solution.py:46
  28.2 3.7 %gather_fusion.3 = f32[512]{0:T(512)S(1)} fusion(f32[128,64]{0,1:T(8,128)S(1)} %copy-done.3, s32[512]{0:T(512)S(1)} %get-tuple-element.85), kind=kCustom, calls=%fused_computation.3 | custom fusion | bytes 8192 | tf_op jit(solution)/shard_map/gather | solution.py:45
  32.0 4.5 %gather_fusion.4 = f32[512]{0:T(512)S(1)} fusion(f32[64,512]{1,0:T(8,128)S(1)} %copy-done.4, s32[512]{0:T(512)S(1)} %get-tuple-element.83), kind=kCustom, calls=%fused_computation.4 | custom fusion | bytes 8192 | tf_op jit(solution)/shard_map/gather | solution.py:45
  36.5 3.3 %fusion.2 = bf16[1,512,2048]{2,1,0:T(8,128)(2,1)} fusion(bf16[512,2048]{1,0:T(8,128)(2,1)} %add_convert_fusion, f32[512]{0:T(512)S(1)} %add_select_fusion), kind=kLoop, calls=%fused_computation.15 | loop fusion | flops 3145728 | bytes 4196352 | tf_op jit(solution)/shard_map/reshape | solution.py:52
  39.8 7.9 %broadcast_in_dim.20 = f32[2048,2048]{1,0:T(8,128)} broadcast(f32[]{:T(128)} %constant.46.clone.1), dimensions={} | broadcast | bytes 16777220 | tf_op jit(solution)/shard_map/broadcast_in_dim | solution.py:66
  47.7 17.3 %while.21 = (s32[]{:T(128)}, f32[2048,2048]{1,0:T(8,128)}, s32[]{:T(128)}, bf16[1,512,2048]{2,1,0:T(8,128)(2,1)}, bf16[1,512,2048]{2,1,0:T(8,128)(2,1)}, /*index=5*/s32[]{:T(128)}) while((s32[]{:T(128)}, f32[2048,2048]{1,0:T(8,128)}, s32[]{:T(128)}, bf16[1,512,2048]{2,1,0:T(8,128)(2,1)}, bf16[1,512,2048]{2,1,0:T(8,128)(2,1)}, ...), condition=%wide.region_5.6_spmd, body=%wide.region_4.5_spmd.sunk | while | flops 4299161600 | bytes 37748804 | solution.py:62
  47.7 17.3 %convolution_add_fusion.2 = f32[2048,2048]{1,0:T(8,128)} fusion(f32[2048,2048]{1,0:T(8,128)} %get-tuple-element.178, bf16[1,512,2048]{2,1,0:T(8,128)(2,1)} %get-tuple-element.187, bf16[1,512,2048]{2,1,0:T(8,128)(2,1)} %get-tuple-element.186), kind=kOutput, calls=%fused_computation.10.clone.1 | convolution fusion | flops 4299161600 | bytes 37748736 | tf_op jit(solution)/shard_map/while/body/dot_general | solution.py:57
  65.1 0.0 reduce-scatter.2.cloned.1.call-update
  65.1 0.0 all-reduce.2.cloned.1.call-start
  65.1 0.1 copy.16
  65.2 125.7 %reduce-scatter.2.cloned.1.call-done = f32[64,2048]{1,0:T(8,128)} async-done(((f32[2048,2048]{1,0:T(8,128)}), f32[64,2048]{1,0:T(8,128)}) %reduce-scatter.2.cloned.1.call-update) | async-done | bytes 524304 | tf_op jit(solution)/shard_map/reduce_scatter | solution.py:61
  191.0 0.0 all-reduce.2.cloned.1.call-update
  191.0 7.2 %while.20 = (s32[]{:T(128)}, f32[4,32,64]{2,1,0:T(8,128)S(1)}, f32[4,32,64]{2,1,0:T(8,128)S(1)}, bf16[4,32,512]{2,1,0:T(8,128)(2,1)}, f32[64,512]{1,0:T(8,128)S(1)}, /*index=5*/s32[]{:T(128)}) while((s32[]{:T(128)}, f32[4,32,64]{2,1,0:T(8,128)S(1)}, f32[4,32,64]{2,1,0:T(8,128)S(1)}, bf16[4,32,512]{2,1,0:T(8,128)(2,1)}, ...), condition=%wide.region_2.3_spmd, body=%wide.region_0.2_spmd.sunk | while | flops 4208642 | bytes 360529 | solution.py:31
  191.0 0.8 bitcast_convert_fusion.2
  191.8 1.0 abs_reduce_fusion.2
  192.8 0.8 bitcast_convert_fusion.2
  193.6 1.0 abs_reduce_fusion.2
  194.6 0.8 bitcast_convert_fusion.2
  195.4 1.0 abs_reduce_fusion.2
  196.4 0.8 bitcast_convert_fusion.2
  197.2 1.0 abs_reduce_fusion.2
  198.2 30.7 %pmax.7 = f32[128,64]{1,0:T(8,128)S(1)} all-reduce(f32[128,64]{1,0:T(8,128)S(1)} %bitcast.35), channel_id=1, replica_groups=mesh['cont'=8,'line'=8,'scen'=4] {'cont'}, use_global_device_ids=true, to_apply=%region_3.4 | all-reduce | flops 8192 | bytes 65536 | tf_op jit(solution)/shard_map/pmax | solution.py:38
  228.9 0.1 broadcast_divide_fusion
  229.0 0.7 copy.17
  229.7 36.6 %all-reduce.2.cloned.1.call-done = f32[64,2048]{1,0:T(8,128)} async-done(((f32[64,2048]{1,0:T(8,128)}), f32[64,2048]{1,0:T(8,128)}) %all-reduce.2.cloned.1.call-update) | async-done | bytes 524304 | tf_op jit(solution)/shard_map/psum | solution.py:72
  266.3 1.9 broadcast_multiply_fusion
  (22 shorter events, 0.1 us)
Async XLA Ops:
  7.2 10.1 %copy-start = (bf16[512,2048]{1,0:T(8,128)(2,1)S(1)}, bf16[512,2048]{1,0:T(8,128)(2,1)}, u32[]{:S(2)}) copy-start(bf16[512,2048]{1,0:T(8,128)(2,1)} %param.19) | copy-start | bytes 6291460
  7.2 6.8 %copy-start.2 = (bf16[128,2048]{1,0:T(8,128)(2,1)S(1)}, bf16[128,2048]{1,0:T(8,128)(2,1)}, u32[]{:S(2)}) copy-start(bf16[128,2048]{1,0:T(8,128)(2,1)} %param.18) | copy-start | bytes 1572868
  7.2 183.8 %reduce-scatter.2.cloned.1.call-start = ((), (), s32[]{:S(2)}) async-start(), calls=%async_computation.1 | async-start | bytes 17301504 | tf_op jit(solution)/shard_map/reduce_scatter | solution.py:61
  20.6 4.2 %copy-start.1 = (f32[128]{0:T(128)S(1)}, f32[128]{0:T(128)}, u32[]{:S(2)}) copy-start(f32[128]{0:T(128)} %param.17) | copy-start | bytes 1540
  24.8 3.4 %copy-start.3 = (f32[128,64]{0,1:T(8,128)S(1)}, f32[128,64]{0,1:T(8,128)}, u32[]{:S(2)}) copy-start(f32[128,64]{0,1:T(8,128)} %param.15) | copy-start | bytes 98308
  24.8 7.1 %copy-start.4 = (f32[64,512]{1,0:T(8,128)S(1)}, f32[64,512]{1,0:T(8,128)}, u32[]{:S(2)}) copy-start(f32[64,512]{1,0:T(8,128)} %param.16) | copy-start | bytes 393220
  65.1 201.2 %all-reduce.2.cloned.1.call-start = ((), (), s32[]{:S(2)}) async-start(), calls=%async_computation.2 | async-start | bytes 1048576 | tf_op jit(solution)/shard_map/psum | solution.py:72
Sparse Core Ops, SparseCore 0:
  65.2 125.7 reduce-scatter.1
  193.3 72.9 all-reduce.1
where the time goes:
time: 276 us; the launch traced here: 275 us
  waiting for transfers between devices  162 us (59%)
  local copies, waits for them, and re-layouts  32.1 us (12%)
  blocking collectives  30.7 us (11%)
  other arithmetic  17.3 us (6%)
  matrix products  17.3 us (6%)
  between operations  15 us (5%)
    reduce_scatter x1, waiting for transfers between devices, local(): lax.psum_scatter(lax.fori_loop(0, trips, step, jnp.zeros((lax.axis_size((...  126 us
    psum x1, waiting for transfers between devices, local(): total = lax.psum(owned, 'cont')  36.6 us
    pmax x1, blocking collectives, local(): worst = lax.pmax(local_worst, 'cont') / limits[:, None]  30.7 us
    dot_general x1, matrix products, step(): lax.dot_general(row_tile, scaled_tile, (((0,), (0,)), ((), ())), preferre...  17.3 us
    gather x2, local copies, waits for them, and re-layouts, local(): post = flow[viol_line, viol_scen] + coef * out_flow[viol_scen, viol_cont]  8.27 us
    broadcast_in_dim x1, local copies, waits for them, and re-layouts, local(): jnp.zeros((lax.axis_size(('line', 'scen')) * (width // owners), width), j...  7.86 us
  transfers between devices with their start and end apart: 2, of which 2 were waited for; matrix products, arithmetic and copies ran while one was open for 3% of the time, Pallas kernels for 0%

commit v1 on v0

--- a/solution.py
+++ b/solution.py
@@ -69,7 +69,7 @@
         scatter_dimension=0,
         tiled=True,
     )
-    total = lax.psum(owned, "cont")
+    total = jnp.sum(lax.all_gather(owned, "cont"), axis=0)
     schur = total * (1.0 / (n_rows * devices))
     return (worst, schur)
 

time: 276 us -> 260 us (0.942)
  waiting for transfers between devices: 162 us -> 144 us
    psum x1 -> x0, waiting for transfers between devices: 36.6 us -> none  [local(): total = lax.psum(owned, 'cont')]
    all_gather x0 -> x1, waiting for transfers between devices: none -> 17.7 us  [local(): total = jnp.sum(lax.all_gather(owned, 'cont'), axis=0)]
where the time goes in v1:
time: 260 us; the launch traced here: 258 us
  waiting for transfers between devices  144 us (55%)
  local copies, waits for them, and re-layouts  32.1 us (12%)
  blocking collectives  31.3 us (12%)
  other arithmetic  18.7 us (7%)
  matrix products  17.3 us (7%)
  between operations  15 us (6%)
    reduce_scatter x1, waiting for transfers between devices, local(): lax.psum_scatter(lax.fori_loop(0, trips, step, jnp.zeros((lax.axis_size((...  126 us
    pmax x1, blocking collectives, local(): worst = lax.pmax(local_worst, 'cont') / limits[:, None]  31.3 us
    all_gather x1, waiting for transfers between devices, local(): total = jnp.sum(lax.all_gather(owned, 'cont'), axis=0)  17.7 us
    dot_general x1, matrix products, step(): lax.dot_general(row_tile, scaled_tile, (((0,), (0,)), ((), ())), preferre...  17.3 us
    gather x2, local copies, waits for them, and re-layouts, local(): post = flow[viol_line, viol_scen] + coef * out_flow[viol_scen, viol_cont]  8.27 us
    broadcast_in_dim x1, local copies, waits for them, and re-layouts, local(): jnp.zeros((lax.axis_size(('line', 'scen')) * (width // owners), width), j...  7.86 us
  transfers between devices with their start and end apart: 2, of which 2 were waited for; matrix products, arithmetic and copies ran while one was open for 3% of the time, Pallas kernels for 0%

profile of v1, /device:TPU:2, one launch (start us, length us, event | category | flops | bytes accessed | tf_op | source)
XLA Modules:
  0.0 258.3 jit_solution(6588818843966024356)
XLA Ops:
  7.2 0.0 reduce-scatter.2.cloned.1.call-start
  8.1 0.7 shift-left_or_fusion
  8.8 5.2 %gather_fusion.1 = bf16[512]{0:T(512)(128)(2,1)S(1)} fusion(bf16[128,512]{1,0:T(8,128)(2,1)} %param.14, s32[512]{0:T(512)S(1)} %get-tuple-element.84), kind=kCustom, calls=%fused_computation.1 | custom fusion | bytes 6144 | tf_op jit(solution)/shard_map/gather | solution.py:39
  14.0 3.3 %gather_fusion = bf16[512,2048]{1,0:T(8,128)(2,1)} fusion(bf16[128,2048]{1,0:T(8,128)(2,1)S(1)} %copy-done.2, s32[1024]{0:T(1024)S(1)} %get-tuple-element.89), kind=kCustom, calls=%fused_computation | custom fusion | bytes 4196352 | tf_op jit(solution)/shard_map/gather | solution.py:41
  17.3 3.3 %gather_fusion.2 = bf16[512,2048]{1,0:T(8,128)(2,1)} fusion(bf16[512,2048]{1,0:T(8,128)(2,1)S(1)} %copy-done, s32[1024]{0:T(1024)S(1)} %get-tuple-element.88), kind=kCustom, calls=%fused_computation.2 | custom fusion | bytes 4196352 | tf_op jit(solution)/shard_map/gather | solution.py:42
  20.6 4.2 %add_convert_fusion = bf16[512,2048]{1,0:T(8,128)(2,1)} fusion(bf16[512,2048]{1,0:T(8,128)(2,1)} %gather_fusion.2, bf16[512,2048]{1,0:T(8,128)(2,1)} %gather_fusion, f32[512]{0:T(512)S(1)} %convert_element_type.36), kind=kLoop, calls=%fused_computation.14 | loop fusion | flops 5242880 | bytes 6293504 | tf_op jit(solution)/shard_map/convert_element_type | solution.py:43
  24.8 3.3 %gather_fusion.5 = f32[512]{0:T(512)S(1)} fusion(f32[128]{0:T(128)S(1)} %copy-done.1, s32[1024]{0:T(1024)S(1)} %get-tuple-element.89), kind=kCustom, calls=%fused_computation.5 | custom fusion | bytes 6144 | tf_op jit(solution)/shard_map/gather | solution.py:46
  28.2 3.7 %gather_fusion.3 = f32[512]{0:T(512)S(1)} fusion(f32[128,64]{0,1:T(8,128)S(1)} %copy-done.3, s32[512]{0:T(512)S(1)} %get-tuple-element.85), kind=kCustom, calls=%fused_computation.3 | custom fusion | bytes 8192 | tf_op jit(solution)/shard_map/gather | solution.py:45
  32.0 4.5 %gather_fusion.4 = f32[512]{0:T(512)S(1)} fusion(f32[64,512]{1,0:T(8,128)S(1)} %copy-done.4, s32[512]{0:T(512)S(1)} %get-tuple-element.83), kind=kCustom, calls=%fused_computation.4 | custom fusion | bytes 8192 | tf_op jit(solution)/shard_map/gather | solution.py:45
  36.5 3.3 %fusion.2 = bf16[1,512,2048]{2,1,0:T(8,128)(2,1)} fusion(bf16[512,2048]{1,0:T(8,128)(2,1)} %add_convert_fusion, f32[512]{0:T(512)S(1)} %add_select_fusion), kind=kLoop, calls=%fused_computation.15 | loop fusion | flops 3145728 | bytes 4196352 | tf_op jit(solution)/shard_map/reshape | solution.py:52
  39.9 7.9 %broadcast_in_dim.20 = f32[2048,2048]{1,0:T(8,128)} broadcast(f32[]{:T(128)} %constant.31.clone.1), dimensions={} | broadcast | bytes 16777220 | tf_op jit(solution)/shard_map/broadcast_in_dim | solution.py:66
  47.7 17.3 %while.21 = (s32[]{:T(128)}, f32[2048,2048]{1,0:T(8,128)}, s32[]{:T(128)}, bf16[1,512,2048]{2,1,0:T(8,128)(2,1)}, bf16[1,512,2048]{2,1,0:T(8,128)(2,1)}, /*index=5*/s32[]{:T(128)}) while((s32[]{:T(128)}, f32[2048,2048]{1,0:T(8,128)}, s32[]{:T(128)}, bf16[1,512,2048]{2,1,0:T(8,128)(2,1)}, bf16[1,512,2048]{2,1,0:T(8,128)(2,1)}, ...), condition=%wide.region_5.6_spmd, body=%wide.region_4.5_spmd.sunk | while | flops 4299161600 | bytes 37748804 | solution.py:62
  47.7 17.3 %convolution_add_fusion.2 = f32[2048,2048]{1,0:T(8,128)} fusion(f32[2048,2048]{1,0:T(8,128)} %get-tuple-element.178, bf16[1,512,2048]{2,1,0:T(8,128)(2,1)} %get-tuple-element.187, bf16[1,512,2048]{2,1,0:T(8,128)(2,1)} %get-tuple-element.186), kind=kOutput, calls=%fused_computation.10.clone.1 | convolution fusion | flops 4299161600 | bytes 37748736 | tf_op jit(solution)/shard_map/while/body/dot_general | solution.py:57
  65.1 0.0 reduce-scatter.2.cloned.1.call-update
  65.1 0.0 all-gather.3.cloned.1.call-start
  65.1 125.9 %reduce-scatter.2.cloned.1.call-done = f32[64,2048]{1,0:T(8,128)} async-done(((f32[2048,2048]{1,0:T(8,128)}), f32[64,2048]{1,0:T(8,128)}) %reduce-scatter.2.cloned.1.call-update) | async-done | bytes 524304 | tf_op jit(solution)/shard_map/reduce_scatter | solution.py:61
  191.0 0.1 copy.16
  191.1 7.2 %while.20 = (s32[]{:T(128)}, f32[4,32,64]{2,1,0:T(8,128)S(1)}, f32[4,32,64]{2,1,0:T(8,128)S(1)}, bf16[4,32,512]{2,1,0:T(8,128)(2,1)}, f32[64,512]{1,0:T(8,128)S(1)}, /*index=5*/s32[]{:T(128)}) while((s32[]{:T(128)}, f32[4,32,64]{2,1,0:T(8,128)S(1)}, f32[4,32,64]{2,1,0:T(8,128)S(1)}, bf16[4,32,512]{2,1,0:T(8,128)(2,1)}, ...), condition=%wide.region_2.3_spmd, body=%wide.region_0.2_spmd.sunk | while | flops 4208642 | bytes 360529 | solution.py:31
  191.1 0.8 bitcast_convert_fusion.2
  191.9 1.0 abs_reduce_fusion.2
  192.9 0.8 bitcast_convert_fusion.2
  193.7 1.0 abs_reduce_fusion.2
  194.7 0.8 bitcast_convert_fusion.2
  195.5 1.0 abs_reduce_fusion.2
  196.5 0.8 bitcast_convert_fusion.2
  197.3 1.0 abs_reduce_fusion.2
  198.3 31.3 %pmax.7 = f32[128,64]{1,0:T(8,128)S(1)} all-reduce(f32[128,64]{1,0:T(8,128)S(1)} %bitcast.37), channel_id=1, replica_groups=mesh['cont'=8,'line'=8,'scen'=4] {'cont'}, use_global_device_ids=true, to_apply=%region_3.4 | all-reduce | flops 8192 | bytes 65536 | tf_op jit(solution)/shard_map/pmax | solution.py:38
  229.6 0.1 broadcast_divide_fusion
  229.7 0.7 copy.17
  230.4 17.7 %all-gather.3.cloned.1.call-done = f32[512,2048]{1,0:T(8,128)} async-done(((f32[64,2048]{1,0:T(8,128)}), f32[512,2048]{1,0:T(8,128)}) %all-gather.3.cloned.1.call-update) | async-done | bytes 4194320 | tf_op jit(solution)/shard_map/all_gather | solution.py:72
  248.1 2.5 reduce_sum.9
  250.6 0.8 broadcast_multiply_fusion
  (23 shorter events, 0.1 us)
Async XLA Ops:
  7.2 10.1 %copy-start = (bf16[512,2048]{1,0:T(8,128)(2,1)S(1)}, bf16[512,2048]{1,0:T(8,128)(2,1)}, u32[]{:S(2)}) copy-start(bf16[512,2048]{1,0:T(8,128)(2,1)} %param.19) | copy-start | bytes 6291460
  7.2 6.8 %copy-start.2 = (bf16[128,2048]{1,0:T(8,128)(2,1)S(1)}, bf16[128,2048]{1,0:T(8,128)(2,1)}, u32[]{:S(2)}) copy-start(bf16[128,2048]{1,0:T(8,128)(2,1)} %param.18) | copy-start | bytes 1572868
  7.2 183.8 %reduce-scatter.2.cloned.1.call-start = ((), (), s32[]{:S(2)}) async-start(), calls=%async_computation.1 | async-start | bytes 17301504 | tf_op jit(solution)/shard_map/reduce_scatter | solution.py:61
  20.6 4.2 %copy-start.1 = (f32[128]{0:T(128)S(1)}, f32[128]{0:T(128)}, u32[]{:S(2)}) copy-start(f32[128]{0:T(128)} %param.17) | copy-start | bytes 1540
  20.6 7.6 %copy-start.3 = (f32[128,64]{0,1:T(8,128)S(1)}, f32[128,64]{0,1:T(8,128)}, u32[]{:S(2)}) copy-start(f32[128,64]{0,1:T(8,128)} %param.15) | copy-start | bytes 98308
  20.6 11.4 %copy-start.4 = (f32[64,512]{1,0:T(8,128)S(1)}, f32[64,512]{1,0:T(8,128)}, u32[]{:S(2)}) copy-start(f32[64,512]{1,0:T(8,128)} %param.16) | copy-start | bytes 393220
  65.1 183.0 %all-gather.3.cloned.1.call-start = ((), (), s32[]{:S(2)}) async-start(), calls=%async_computation.2 | async-start | bytes 4718592 | tf_op jit(solution)/shard_map/all_gather | solution.py:72
Sparse Core Ops, SparseCore 0:
  65.2 125.7 reduce-scatter.1
  192.8 55.2 all-gather.2
